TPU v7x, 256 devices: a whole 4x4x8 slice. The times are simulated.
256 devices in a mesh: in: 4 (over y_hi, core), out: 8 (over y_lo, x), depth: 8 (over z).
Axes of the slice: x: 4, y: 4 (y_hi: 2, y_lo: 2; y = y_hi * 2 + y_lo), z: 8, core: 2. Of those that a mesh axis runs over, the one named last changes fastest.
Arguments:
- inputs: bfloat16 [4096, 6144], P(('depth', 'out'), 'in'), may hold values from -6 to 6
- weight: bfloat16 [6144, 24576], P(('in', 'depth'), 'out'), may hold values from -0.078125 to 0.078125
- cotangent: bfloat16 [4096, 24576], P(('depth', 'in'), 'out'), may hold values from -6 to 6
Outputs:
- activated: bfloat16 [4096, 24576], P(('depth', 'in'), 'out')
- grad_inputs: bfloat16 [4096, 6144], P(('depth', 'out'), 'in')
- grad_weight: bfloat16 [6144, 24576], P(('in', 'depth'), 'out')
All inputs are finite; a program needn't handle non-finite values.
Results may differ from a plain program's by a relative error of at most 0.005.
Values may be sent and summed in bfloat16 or wider, within the bound.
No kernel may reach another device: no remote copies, remote signals or barrier semaphores. Data moves between devices by JAX's collectives and lax.ppermute only.
A program may use at most 128 MiB of HBM per device.

v0:
```python
import math

import jax
import jax.numpy as jnp
from jax import lax
from jax.sharding import PartitionSpec as P

slope_c = math.sqrt(2.0 / math.pi)


def gelu_tanh(value):
    inner = slope_c * (value + 0.044715 * value * value * value)
    return 0.5 * value * (1.0 + jnp.tanh(inner))


def gelu_slope(value):
    inner = slope_c * (value + 0.044715 * value * value * value)
    tangent = jnp.tanh(inner)
    return 0.5 * (1.0 + tangent) + 0.5 * value * (1.0 - tangent * tangent) * slope_c * (
        1.0 + 3.0 * 0.044715 * value * value
    )


def body(inputs, weight, cotangent):
    x_group = lax.all_gather(inputs, "out", axis=0, tiled=True)
    w_block = lax.all_gather(weight, "depth", axis=0, tiled=True)
    row_block = x_group
    pre_act = lax.psum_scatter(
        jnp.dot(row_block, w_block, preferred_element_type=jnp.float32),
        "in",
        scatter_dimension=0,
        tiled=True,
    )
    activated = gelu_tanh(pre_act).astype(jnp.bfloat16)
    d_hidden = (cotangent.astype(jnp.float32) * gelu_slope(pre_act)).astype(jnp.bfloat16)
    dh_group = lax.all_gather(d_hidden, "in", axis=0, tiled=True)
    row_block = dh_group
    grad_inputs = lax.psum_scatter(
        lax.dot_general(
            row_block, w_block, (((1,), (1,)), ((), ())), preferred_element_type=jnp.float32
        ),
        "out",
        scatter_dimension=0,
        tiled=True,
    ).astype(jnp.bfloat16)
    grad_weight = lax.psum_scatter(
        lax.dot_general(
            x_group, dh_group, (((0,), (0,)), ((), ())), preferred_element_type=jnp.float32
        ),
        "depth",
        scatter_dimension=0,
        tiled=True,
    ).astype(jnp.bfloat16)
    return (activated, grad_inputs, grad_weight)


def solution(mesh):
    in_specs = (P(("depth", "out"), "in"), P(("in", "depth"), "out"), P(("depth", "in"), "out"))
    out_specs = (P(("depth", "in"), "out"), P(("depth", "out"), "in"), P(("in", "depth"), "out"))
    return jax.shard_map(body, mesh=mesh, in_specs=in_specs, out_specs=out_specs, check_vma=False)
```

profile of v0, /device:TPU:1, one launch (start us, length us, event | category | flops | bytes accessed | tf_op | source)
XLA Modules:
  0.0 543.9 jit_solution(2217947623932337867)
XLA Ops:
  7.2 0.0 all-gather.4.cloned.1.call-start
  7.2 0.7 all-gather.4.cloned.1.call-update
  7.9 0.0 all-gather.6.cloned.1.call-start
  7.9 0.7 all-gather.6.cloned.1.call-update
  8.6 0.0 reduce-scatter.6.cloned.1.call-start
  8.7 41.8 %all-gather.4.cloned.1.call-done = bf16[512,1536]{1,0:T(8,128)(2,1)} async-done(((bf16[64,1536]{1,0:T(8,128)(2,1)}), bf16[512,1536]{1,0:T(8,128)(2,1)}) %all-gather.4.cloned.1.call-update) | async-done | bytes 1572880 | tf_op jit(solution)/shard_map/all_gather | solution.py:25
  50.5 111.2 %all-gather.6.cloned.1.call-done = bf16[1536,3072]{1,0:T(8,128)(2,1)} async-done(((bf16[192,3072]{1,0:T(8,128)(2,1)}), bf16[1536,3072]{1,0:T(8,128)(2,1)}) %all-gather.6.cloned.1.call-update) | async-done | bytes 9437200 | tf_op jit(solution)/shard_map/all_gather | solution.py:26
  161.7 9.9 %fusion.7 = f32[512,3072]{1,0:T(8,128)} fusion(bf16[512,1536]{1,0:T(8,128)(2,1)} %all-gather.4.cloned.1.call-done, bf16[1536,3072]{1,0:T(8,128)(2,1)} %all-gather.6.cloned.1.call-done), kind=kOutput, calls=%fused_computation.11 | convolution fusion | flops 4831838208 | bytes 17301504 | tf_op jit(solution)/shard_map/dot_general | solution.py:29
  171.6 0.0 copy-start
  171.6 0.0 reduce-scatter.6.cloned.1.call-update
  171.6 0.0 all-gather.8.cloned.1.call-start
  171.7 69.1 %reduce-scatter.6.cloned.1.call-done = f32[128,3072]{1,0:T(8,128)} async-done(((f32[512,3072]{1,0:T(8,128)}), f32[128,3072]{1,0:T(8,128)}) %reduce-scatter.6.cloned.1.call-update) | async-done | bytes 1572880 | tf_op jit(solution)/shard_map/reduce_scatter | solution.py:28
  240.8 0.0 copy-done
  240.8 3.7 fusion.6
  244.5 0.0 all-gather.8.cloned.1.call-update
  244.5 0.0 reduce-scatter.8.cloned.1.call-start
  244.6 35.1 %all-gather.8.cloned.1.call-done = bf16[512,3072]{1,0:T(8,128)(2,1)} async-done(((bf16[128,3072]{1,0:T(8,128)(2,1)}), bf16[512,3072]{1,0:T(8,128)(2,1)}) %all-gather.8.cloned.1.call-update) | async-done | bytes 3145744 | tf_op jit(solution)/shard_map/all_gather | solution.py:36
  279.7 10.6 %fusion.8 = f32[512,1536]{1,0:T(8,128)} fusion(bf16[512,3072]{1,0:T(8,128)(2,1)} %all-gather.8.cloned.1.call-done, bf16[1536,3072]{1,0:T(8,128)(2,1)} %all-gather.6.cloned.1.call-done), kind=kOutput, calls=%fused_computation.12 | convolution fusion | flops 4831838208 | bytes 15728640 | tf_op jit(solution)/shard_map/dot_general | solution.py:39
  290.3 0.0 copy-start.1
  290.3 0.0 reduce-scatter.8.cloned.1.call-update
  290.3 0.0 reduce-scatter.10.cloned.1.call-start
  290.3 1.8 copy-done.1
  292.2 10.8 %convolution_bitcast_fusion = f32[1536,3072]{0,1:T(8,128)} fusion(bf16[512,3072]{1,0:T(8,128)(2,1)S(1)} %copy-done.1, bf16[512,1536]{1,0:T(8,128)(2,1)} %all-gather.4.cloned.1.call-done), kind=kOutput, calls=%fused_computation | convolution fusion | flops 4831838208 | bytes 23592960 | tf_op jit(solution)/shard_map/dot_general | solution.py:47
  303.0 18.7 %copy.8 = f32[1536,3072]{1,0:T(8,128)} copy(f32[1536,3072]{0,1:T(8,128)} %convolution_bitcast_fusion) | data formatting | bytes 37748736
  321.7 0.0 reduce-scatter.10.cloned.1.call-update
  321.8 12.3 %reduce-scatter.8.cloned.1.call-done = f32[64,1536]{1,0:T(8,128)} async-done(((f32[512,1536]{1,0:T(8,128)}), f32[64,1536]{1,0:T(8,128)}) %reduce-scatter.8.cloned.1.call-update) | async-done | bytes 393232 | tf_op jit(solution)/shard_map/reduce_scatter | solution.py:38
  334.1 1.7 convert_element_type.18
  335.8 197.9 %reduce-scatter.10.cloned.1.call-done = f32[192,3072]{1,0:T(8,128)} async-done(((f32[1536,3072]{1,0:T(8,128)}), f32[192,3072]{1,0:T(8,128)}) %reduce-scatter.10.cloned.1.call-update) | async-done | bytes 2359312
  533.6 1.9 copy.9
  535.6 1.5 copy.7
Async XLA Ops:
  7.2 43.4 %all-gather.4.cloned.1.call-start = ((), (), s32[]{:S(2)}) async-start(), calls=%async_computation.3 | async-start | bytes 1769472 | tf_op jit(solution)/shard_map/all_gather | solution.py:25
  7.9 153.8 %all-gather.6.cloned.1.call-start = ((), (), s32[]{:S(2)}) async-start(), calls=%async_computation.4 | async-start | bytes 10616832 | tf_op jit(solution)/shard_map/all_gather | solution.py:26
  8.6 232.2 %reduce-scatter.6.cloned.1.call-start = ((), (), s32[]{:S(2)}) async-start(), calls=%async_computation.5 | async-start | bytes 7864320 | tf_op jit(solution)/shard_map/reduce_scatter | solution.py:28
  171.6 69.2 %copy-start = (bf16[128,3072]{1,0:T(8,128)(2,1)S(1)}, bf16[128,3072]{1,0:T(8,128)(2,1)}, u32[]{:S(2)}) copy-start(bf16[128,3072]{1,0:T(8,128)(2,1)} %param.5) | copy-start | bytes 2359300
  171.6 108.0 %all-gather.8.cloned.1.call-start = ((), (), s32[]{:S(2)}) async-start(), calls=%async_computation.6 | async-start | bytes 3932160 | tf_op jit(solution)/shard_map/all_gather | solution.py:36
  244.5 89.6 %reduce-scatter.8.cloned.1.call-start = ((), (), s32[]{:S(2)}) async-start(), calls=%async_computation.7 | async-start | bytes 3538944 | tf_op jit(solution)/shard_map/reduce_scatter | solution.py:38
  290.3 1.9 copy-start.1
  290.3 243.3 %reduce-scatter.10.cloned.1.call-start = ((), (), s32[]{:S(2)}) async-start(), calls=%async_computation.8 | async-start | bytes 21233664
Sparse Core Ops, SparseCore 0:
  9.8 40.6 all-gather.3
  52.3 109.3 all-gather.5
  171.8 69.0 reduce-scatter.5
  244.6 34.9 all-gather.7
  290.4 43.6 reduce-scatter.7
  336.7 196.8 reduce-scatter.9
where the time goes:
time: 544 us
  waiting for transfers between devices  469 us (86%)
  matrix products  31.3 us (6%)
  local copies, waits for them, and re-layouts  23.9 us (4%)
  between operations  14.1 us (3%)
    unnamed x7, waiting for transfers between devices  199 us
    all_gather x1, waiting for transfers between devices, body(): w_block = lax.all_gather(weight, 'depth', axis=0, tiled=True)  111 us
    reduce_scatter x1, waiting for transfers between devices, body(): lax.psum_scatter(jnp.dot(row_block, w_block, preferred_element_type=jnp.f...  69.1 us
    all_gather x1, waiting for transfers between devices, body(): x_group = lax.all_gather(inputs, 'out', axis=0, tiled=True)  41.8 us
    all_gather x1, waiting for transfers between devices, body(): dh_group = lax.all_gather(d_hidden, 'in', axis=0, tiled=True)  35.1 us
    unnamed x7, local copies, waits for them, and re-layouts  23.9 us
    reduce_scatter x1, waiting for transfers between devices, body(): lax.psum_scatter(lax.dot_general(row_block, w_block, (((1,), (1,)), ((),...  12.3 us
  transfers between devices with their start and end apart: 6, of which 6 were waited for; matrix products, arithmetic and copies ran while one was open for 6% of the time, Pallas kernels for 0%

commit v1 on v0

v1 whole, which is shorter than its diff:
```python
import math

import jax
import jax.numpy as jnp
from jax import lax
from jax.sharding import PartitionSpec as P

slope_c = math.sqrt(2.0 / math.pi)
CHUNKS = 4


def gelu_both(value):
    inner = slope_c * (value + 0.044715 * value * value * value)
    t = jnp.tanh(inner)
    act = 0.5 * value * (1.0 + t)
    slope = 0.5 * (1.0 + t) + 0.5 * value * (1.0 - t * t) * slope_c * (
        1.0 + 3.0 * 0.044715 * value * value
    )
    return act, slope


def mm(a, b):
    return jnp.dot(a, b, preferred_element_type=jnp.float32)


def body(inputs, weight, cotangent):
    nz = lax.axis_size("depth")
    z = lax.axis_index("depth")
    i = lax.axis_index("in")
    up = [(s, (s + 1) % nz) for s in range(nz)]
    down = [(s, (s - 1) % nz) for s in range(nz)]
    core = [(s, s ^ 1) for s in range(4)]
    yhi = [(s, s ^ 2) for s in range(4)]
    send = lax.ppermute

    wr = weight.shape[0]
    half = wr // 2
    fc = weight.shape[1] // CHUNKS
    rows = cotangent.shape[0]

    doubled = jnp.concatenate([inputs, inputs], axis=1)
    x_local = lax.dynamic_slice_in_dim(doubled, z * wr, inputs.shape[1], axis=1)
    x_group = lax.all_gather(x_local, "out", axis=0, tiled=True)
    blocks = [lax.dynamic_slice_in_dim(x_group, (i ^ k) * rows, rows, axis=0) for k in (0, 2, 1, 3)]
    x = jnp.concatenate(blocks, axis=0)
    xt = lax.optimization_barrier(x.T)

    grad_in = None
    acts, grads = [], []
    for c in range(CHUNKS):
        cols = slice(c * fc, (c + 1) * fc)
        own = weight[:, cols]
        u1, d1 = send(own, "depth", up), send(own, "depth", down)
        u2, d2 = send(u1, "depth", up), send(d1, "depth", down)
        u3, d3 = send(u2, "depth", up), send(d2, "depth", down)
        u4, d4 = send(u3[:half], "depth", up), send(d3[half:], "depth", down)
        w = jnp.concatenate([own, d1, d2, d3, u4, d4, u3, u2, u1], axis=0)
        pre = mm(x, w)
        pre = pre[: 2 * rows] + send(pre[2 * rows :], "in", core)
        pre = pre[:rows] + send(pre[rows:], "in", yhi)
        act, slope = gelu_both(pre)
        acts.append(act.astype(jnp.bfloat16))
        dh = (cotangent[:, cols].astype(jnp.float32) * slope).astype(jnp.bfloat16)
        dh = jnp.concatenate([dh, send(dh, "in", yhi)], axis=0)
        dh = jnp.concatenate([dh, send(dh, "in", core)], axis=0)
        gi = lax.dot_general(dh, w, (((1,), (1,)), ((), ())), preferred_element_type=jnp.float32)
        grad_in = gi if grad_in is None else grad_in + gi

        def part(k, dh=dh):
            return mm(xt[k * wr : (k + 1) * wr], dh)

        b16 = jnp.bfloat16
        far = part(4).astype(b16)
        u, d = send(far[:half], "depth", up), send(far[half:], "depth", down)
        pu, pd = part(3), part(5)
        u = jnp.concatenate([pu[:half] + u, pu[half:]], axis=0).astype(b16)
        d = jnp.concatenate([pd[:half], pd[half:] + d], axis=0).astype(b16)
        u, d = send(u, "depth", up), send(d, "depth", down)
        u, d = (part(2) + u).astype(b16), (part(6) + d).astype(b16)
        u, d = send(u, "depth", up), send(d, "depth", down)
        u, d = (part(1) + u).astype(b16), (part(7) + d).astype(b16)
        u, d = send(u, "depth", up), send(d, "depth", down)
        grads.append((part(0) + u + d).astype(b16))

    order = jnp.stack([grad_in[k * rows : (k + 1) * rows] for k in (0, 2, 1, 3)])
    natural = jnp.concatenate(
        [lax.dynamic_index_in_dim(order, k ^ i, axis=0, keepdims=False) for k in range(4)], axis=0
    )
    g = lax.psum_scatter(natural, "out", scatter_dimension=0, tiled=True)
    g = jnp.concatenate([g, g], axis=1)
    g = lax.dynamic_slice_in_dim(g, (nz - z) % nz * wr, inputs.shape[1], axis=1)
    return (
        jnp.concatenate(acts, axis=1),
        g.astype(jnp.bfloat16),
        jnp.concatenate(grads, axis=1),
    )


def solution(mesh):
    in_specs = (P(("depth", "out"), "in"), P(("in", "depth"), "out"), P(("depth", "in"), "out"))
    out_specs = (P(("depth", "in"), "out"), P(("depth", "out"), "in"), P(("in", "depth"), "out"))
    return jax.shard_map(body, mesh=mesh, in_specs=in_specs, out_specs=out_specs, check_vma=False)
```

time: 544 us -> 336 us (0.62); the launches traced: 544 us -> 330 us
  waiting for transfers between devices: 469 us -> 123 us
  starting transfers between devices: 0.24 us -> 108 us
  local copies, waits for them, and re-layouts: 23.9 us -> 41 us
  other arithmetic: 5.36 us -> 16.5 us
  matrix products: 31.3 us -> 25.6 us
    unnamed x7 -> x2, waiting for transfers between devices: 199 us -> 0.03 us
    all_gather x3 -> x1, waiting for transfers between devices: 188 us -> 0.02 us  [body(): x_group = lax.all_gather(x_local, 'out', axis=0, tiled=True)]
    ppermute x0 -> x80, waiting for transfers between devices: none -> 123 us  [the longest x24 46.7 us: body(): u, d = (send(u, 'depth', up), send(d, 'depth', down))]
    ppermute x0 -> x80, starting transfers between devices: none -> 108 us  [the longest x24 21 us: body(): u, d = (send(u, 'depth', up), send(d, 'depth', down))]
    reduce_scatter x2 -> x1, waiting for transfers between devices: 81.5 us -> 0.01 us  [body(): g = lax.psum_scatter(natural, 'out', scatter_dimension=0, tiled=True)]
    slice x0 -> x29, local copies, waits for them, and re-layouts: none -> 8.05 us  [the longest x4 3.12 us: body(): pre = pre[:rows] + send(pre[rows:], 'in', yhi)]
    concatenate x0 -> x16, other arithmetic: none -> 6.06 us  [the longest x1 1.88 us: body(): jnp.concatenate([lax.dynamic_index_in_dim(order, k ^ i, axis=0, keepdims=...]
    dot_general x3 -> x40, matrix products: 31.3 us -> 25.6 us  [the longest x36 19.8 us: mm(): return jnp.dot(a, b, preferred_element_type=jnp.float32)]
  transfers between devices with their start and end apart: 6 -> 82, of which waited for: 6 -> 39; matrix products, arithmetic and copies ran while one was open for 6% -> 20% of each run, Pallas kernels for 0% -> 0%
where the time goes in v1:
time: 336 us; the launch traced here: 330 us
  waiting for transfers between devices  123 us (37%)
  starting transfers between devices  108 us (32%)
  local copies, waits for them, and re-layouts  41 us (12%)
  matrix products  25.6 us (8%)
  other arithmetic  16.5 us (5%)
  between operations  15.6 us (5%)
    ppermute x24, waiting for transfers between devices, body(): u, d = (send(u, 'depth', up), send(d, 'depth', down))  46.7 us
    ppermute x4, waiting for transfers between devices, body(): pre = pre[:rows] + send(pre[rows:], 'in', yhi)  28.8 us
    unnamed x126, local copies, waits for them, and re-layouts  25 us
    ppermute x24, starting transfers between devices, body(): u, d = (send(u, 'depth', up), send(d, 'depth', down))  21 us
    dot_general x36, matrix products, mm(): return jnp.dot(a, b, preferred_element_type=jnp.float32)  19.8 us
    ppermute x8, starting transfers between devices, body(): u4, d4 = (send(u3[:half], 'depth', up), send(d3[half:], 'depth', down))  19.8 us
    ppermute x8, waiting for transfers between devices, body(): u3, d3 = (send(u2, 'depth', up), send(d2, 'depth', down))  15.9 us
    ppermute x8, waiting for transfers between devices, body(): u2, d2 = (send(u1, 'depth', up), send(d1, 'depth', down))  13.4 us
  transfers between devices with their start and end apart: 82, of which 39 were waited for; matrix products, arithmetic and copies ran while one was open for 20% of the time, Pallas kernels for 0%

profile of v1, /device:TPU:1, one launch (start us, length us, event | category | flops | bytes accessed | tf_op | source)
XLA Modules:
  0.0 329.7 jit_solution(2847476983747547048)
XLA Ops:
  9.4 6.4 %collective-permute-start.20 = (bf16[192,768]{1,0:T(8,128)(2,1)S(1)}, bf16[192,768]{1,0:T(8,128)(2,1)}, u32[]{:S(2)}, u32[]{:S(2)}) collective-permute-start(bf16[192,768]{1,0:T(8,128)(2,1)S(1)} %get-tuple-element.30), channel_id=1, source_target_pairs={{0,7},{1,0},{2,1},{3,2},{4,3},{5,4},{6,5},{7,6},{8,15},{9,8},{10,9... | collective-permute-start | bytes 884744 | tf_op jit(solution)/shard_map/ppermute | solution.py:53
  21.5 3.2 collective-permute-done.23
  46.9 3.0 collective-permute-done.24
  53.2 3.0 collective-permute-done.34
  59.5 3.4 %collective-permute-start.32 = (bf16[192,768]{1,0:T(8,128)(2,1)S(1)}, bf16[192,768]{1,0:T(8,128)(2,1)S(1)}, u32[]{:S(2)}, u32[]{:S(2)}) collective-permute-start(bf16[192,768]{1,0:T(8,128)(2,1)S(1)} %collective-permute-done.31), channel_id=1, source_target_pairs={{0,7},{1,0},{2,1},{3,2},{4,3},{5,4},{6,5},{7,6},{8,15},{9,8},{10,9... | collective-permute-start | bytes 884744 | tf_op jit(solution)/shard_map/ppermute | solution.py:55
  65.8 3.5 %collective-permute-start.12 = (bf16[192,768]{1,0:T(8,128)(2,1)S(1)}, bf16[192,768]{1,0:T(8,128)(2,1)S(1)}, u32[]{:S(2)}, u32[]{:S(2)}) collective-permute-start(bf16[192,768]{1,0:T(8,128)(2,1)S(1)} %collective-permute-done.11), channel_id=1, source_target_pairs={{0,7},{1,0},{2,1},{3,2},{4,3},{5,4},{6,5},{7,6},{8,15},{9,8},{10,9... | collective-permute-start | bytes 884744 | tf_op jit(solution)/shard_map/ppermute | solution.py:55
  75.2 3.2 collective-permute-done.32
  79.2 5.6 %collective-permute-done.12 = bf16[192,768]{1,0:T(8,128)(2,1)S(1)} collective-permute-done((bf16[192,768]{1,0:T(8,128)(2,1)S(1)}, bf16[192,768]{1,0:T(8,128)(2,1)S(1)}, u32[]{:S(2)}, u32[]{:S(2)}) %collective-permute-start.12) | collective-permute-done | bytes 294944 | tf_op jit(solution)/shard_map/ppermute | solution.py:55
  85.5 3.5 %collective-permute-start.27 = (bf16[96,768]{1,0:T(8,128)(2,1)S(1)}, bf16[96,768]{1,0:T(8,128)(2,1)S(1)}, u32[]{:S(2)}, u32[]{:S(2)}) collective-permute-start(bf16[96,768]{1,0:T(8,128)(2,1)S(1)} %slice.317), channel_id=1, source_target_pairs={{0,7},{1,0},{2,1},{3,2},{4,3},{5,4},{6,5},{7,6},{8,15},{9,8},{10,9... | collective-permute-start | bytes 442376 | tf_op jit(solution)/shard_map/ppermute | solution.py:56
  91.1 3.5 %collective-permute-start.37 = (bf16[96,768]{1,0:T(8,128)(2,1)S(1)}, bf16[96,768]{1,0:T(8,128)(2,1)S(1)}, u32[]{:S(2)}, u32[]{:S(2)}) collective-permute-start(bf16[96,768]{1,0:T(8,128)(2,1)S(1)} %slice.323), channel_id=1, source_target_pairs={{0,7},{1,0},{2,1},{3,2},{4,3},{5,4},{6,5},{7,6},{8,15},{9,8},{10,9... | collective-permute-start | bytes 442376 | tf_op jit(solution)/shard_map/ppermute | solution.py:56
  98.2 8.5 %collective-permute-start.6 = (bf16[96,768]{1,0:T(8,128)(2,1)S(1)}, bf16[96,768]{1,0:T(8,128)(2,1)S(1)}, u32[]{:S(2)}, u32[]{:S(2)}) collective-permute-start(bf16[96,768]{1,0:T(8,128)(2,1)S(1)} %slice.304), channel_id=1, source_target_pairs={{0,1},{1,2},{2,3},{3,4},{4,5},{5,6},{6,7},{7,0},{8,9},{9,10},{10,1... | collective-permute-start | bytes 442376 | tf_op jit(solution)/shard_map/ppermute | solution.py:56
  126.9 7.2 %collective-permute-start.28 = (f32[256,768]{1,0:T(8,128)S(1)}, f32[256,768]{1,0:T(8,128)S(1)}, u32[]{:S(2)}, u32[]{:S(2)}) collective-permute-start(f32[256,768]{1,0:T(8,128)S(1)} %slice.319), channel_id=1, source_target_pairs={{0,64},{64,0},{128,192},{192,128},{1,65},{65,1},{129,193},{193,129... | collective-permute-start | bytes 2359304 | tf_op jit(solution)/shard_map/ppermute | solution.py:59
  140.3 2.9 collective-permute-start.29
  145.0 2.9 collective-permute-start.19
  148.9 3.5 %collective-permute-done.29 = f32[128,768]{1,0:T(8,128)} collective-permute-done((f32[128,768]{1,0:T(8,128)}, f32[128,768]{1,0:T(8,128)}, u32[]{:S(2)}, u32[]{:S(2)}) %collective-permute-start.29) | collective-permute-done | bytes 393248 | tf_op jit(solution)/shard_map/ppermute | solution.py:60
  152.4 8.4 %collective-permute-done.39 = f32[128,768]{1,0:T(8,128)} collective-permute-done((f32[128,768]{1,0:T(8,128)}, f32[128,768]{1,0:T(8,128)}, u32[]{:S(2)}, u32[]{:S(2)}) %collective-permute-start.39) | collective-permute-done | bytes 393248 | tf_op jit(solution)/shard_map/ppermute | solution.py:60
  160.8 8.4 %collective-permute-done.19 = f32[128,768]{1,0:T(8,128)} collective-permute-done((f32[128,768]{1,0:T(8,128)}, f32[128,768]{1,0:T(8,128)}, u32[]{:S(2)}, u32[]{:S(2)}) %collective-permute-start.19) | collective-permute-done | bytes 393248 | tf_op jit(solution)/shard_map/ppermute | solution.py:60
  169.3 8.4 %collective-permute-done.9 = f32[128,768]{1,0:T(8,128)} collective-permute-done((f32[128,768]{1,0:T(8,128)}, f32[128,768]{1,0:T(8,128)}, u32[]{:S(2)}, u32[]{:S(2)}) %collective-permute-start.9) | collective-permute-done | bytes 393248 | tf_op jit(solution)/shard_map/ppermute | solution.py:60
  180.6 3.2 collective-permute-start.40
  187.6 3.2 collective-permute-start.41
  204.8 3.3 %collective-permute-start.52 = (bf16[96,768]{1,0:T(8,128)(2,1)}, bf16[96,768]{1,0:T(8,128)(2,1)}, u32[]{:S(2)}, u32[]{:S(2)}) collective-permute-start(bf16[96,768]{1,0:T(8,128)(2,1)} %get-tuple-element.38), channel_id=1, source_target_pairs={{0,7},{1,0},{2,1},{3,2},{4,3},{5,4},{6,5},{7,6},{8,15},{9,8},{10,9... | collective-permute-start | bytes 442376 | tf_op jit(solution)/shard_map/ppermute | solution.py:74
  252.9 3.3 collective-permute-done.57
  258.5 4.0 %collective-permute-done.65 = bf16[192,768]{1,0:T(8,128)(2,1)S(1)} collective-permute-done((bf16[192,768]{1,0:T(8,128)(2,1)S(1)}, bf16[192,768]{1,0:T(8,128)(2,1)S(1)}, u32[]{:S(2)}, u32[]{:S(2)}) %collective-permute-start.65) | collective-permute-done | bytes 294944 | tf_op jit(solution)/shard_map/ppermute | solution.py:78
  264.8 4.0 %collective-permute-done.73 = bf16[192,768]{1,0:T(8,128)(2,1)S(1)} collective-permute-done((bf16[192,768]{1,0:T(8,128)(2,1)S(1)}, bf16[192,768]{1,0:T(8,128)(2,1)S(1)}, u32[]{:S(2)}, u32[]{:S(2)}) %collective-permute-start.73) | collective-permute-done | bytes 294944 | tf_op jit(solution)/shard_map/ppermute | solution.py:78
  271.1 4.1 %collective-permute-done.50 = bf16[192,768]{1,0:T(8,128)(2,1)S(1)} collective-permute-done((bf16[192,768]{1,0:T(8,128)(2,1)S(1)}, bf16[192,768]{1,0:T(8,128)(2,1)S(1)}, u32[]{:S(2)}, u32[]{:S(2)}) %collective-permute-start.50) | collective-permute-done | bytes 294944 | tf_op jit(solution)/shard_map/ppermute | solution.py:80
  277.6 3.7 %collective-permute-done.58 = bf16[192,768]{1,0:T(8,128)(2,1)S(1)} collective-permute-done((bf16[192,768]{1,0:T(8,128)(2,1)S(1)}, bf16[192,768]{1,0:T(8,128)(2,1)S(1)}, u32[]{:S(2)}, u32[]{:S(2)}) %collective-permute-start.58) | collective-permute-done | bytes 294944 | tf_op jit(solution)/shard_map/ppermute | solution.py:80
  284.1 3.6 %collective-permute-done.66 = bf16[192,768]{1,0:T(8,128)(2,1)S(1)} collective-permute-done((bf16[192,768]{1,0:T(8,128)(2,1)S(1)}, bf16[192,768]{1,0:T(8,128)(2,1)S(1)}, u32[]{:S(2)}, u32[]{:S(2)}) %collective-permute-start.66) | collective-permute-done | bytes 294944 | tf_op jit(solution)/shard_map/ppermute | solution.py:80
  290.2 3.8 %collective-permute-done.74 = bf16[192,768]{1,0:T(8,128)(2,1)S(1)} collective-permute-done((bf16[192,768]{1,0:T(8,128)(2,1)S(1)}, bf16[192,768]{1,0:T(8,128)(2,1)S(1)}, u32[]{:S(2)}, u32[]{:S(2)}) %collective-permute-start.74) | collective-permute-done | bytes 294944 | tf_op jit(solution)/shard_map/ppermute | solution.py:80
  296.5 3.8 %collective-permute-done.51 = bf16[192,768]{1,0:T(8,128)(2,1)S(1)} collective-permute-done((bf16[192,768]{1,0:T(8,128)(2,1)S(1)}, bf16[192,768]{1,0:T(8,128)(2,1)S(1)}, u32[]{:S(2)}, u32[]{:S(2)}) %collective-permute-start.51) | collective-permute-done | bytes 294944 | tf_op jit(solution)/shard_map/ppermute | solution.py:82
  302.1 4.5 %collective-permute-done.59 = bf16[192,768]{1,0:T(8,128)(2,1)S(1)} collective-permute-done((bf16[192,768]{1,0:T(8,128)(2,1)S(1)}, bf16[192,768]{1,0:T(8,128)(2,1)S(1)}, u32[]{:S(2)}, u32[]{:S(2)}) %collective-permute-start.59) | collective-permute-done | bytes 294944 | tf_op jit(solution)/shard_map/ppermute | solution.py:82
  307.0 6.0 %collective-permute-done.67 = bf16[192,768]{1,0:T(8,128)(2,1)S(1)} collective-permute-done((bf16[192,768]{1,0:T(8,128)(2,1)S(1)}, bf16[192,768]{1,0:T(8,128)(2,1)S(1)}, u32[]{:S(2)}, u32[]{:S(2)}) %collective-permute-start.67) | collective-permute-done | bytes 294944 | tf_op jit(solution)/shard_map/ppermute | solution.py:82
  313.3 6.0 %collective-permute-done.75 = bf16[192,768]{1,0:T(8,128)(2,1)S(1)} collective-permute-done((bf16[192,768]{1,0:T(8,128)(2,1)S(1)}, bf16[192,768]{1,0:T(8,128)(2,1)S(1)}, u32[]{:S(2)}, u32[]{:S(2)}) %collective-permute-start.75) | collective-permute-done | bytes 294944 | tf_op jit(solution)/shard_map/ppermute | solution.py:82
  (368 shorter events, 169.0 us)
Async XLA Ops:
  7.2 115.3 %all-gather.2.cloned.1.call-start = ((), (), s32[]{:S(2)}) async-start(), calls=%async_computation.1 | async-start | bytes 1769472 | tf_op jit(solution)/shard_map/all_gather | solution.py:43
  26.9 293.9 %reduce-scatter.2.cloned.1.call-start = ((), (), s32[]{:S(2)}) async-start(), calls=%async_computation.2 | async-start | bytes 3538944 | tf_op jit(solution)/shard_map/reduce_scatter | solution.py:89
  43.6 16.0 %collective-permute-start.11 = (bf16[192,768]{1,0:T(8,128)(2,1)}, bf16[192,768]{1,0:T(8,128)(2,1)S(1)}, u32[]{:S(2)}, u32[]{:S(2)}) collective-permute-start(bf16[192,768]{1,0:T(8,128)(2,1)} %collective-permute-done.10), channel_id=1, source_target_pairs={{0,7},{1,0},{2,1},{3,2},{4,3},{5,4},{6,5},{7,6},{8,15},{9,8},{10,9... | collective-permute-start | bytes 884744 | tf_op jit(solution)/shard_map/ppermute | solution.py:54
  46.9 16.1 %collective-permute-start.14 = (bf16[192,768]{1,0:T(8,128)(2,1)}, bf16[192,768]{1,0:T(8,128)(2,1)S(1)}, u32[]{:S(2)}, u32[]{:S(2)}) collective-permute-start(bf16[192,768]{1,0:T(8,128)(2,1)} %collective-permute-done.13), channel_id=1, source_target_pairs={{0,1},{1,2},{2,3},{3,4},{4,5},{5,6},{6,7},{7,0},{8,9},{9,10},{10,1... | collective-permute-start | bytes 884744 | tf_op jit(solution)/shard_map/ppermute | solution.py:54
  53.2 16.1 %collective-permute-start.4 = (bf16[192,768]{1,0:T(8,128)(2,1)S(1)}, bf16[192,768]{1,0:T(8,128)(2,1)S(1)}, u32[]{:S(2)}, u32[]{:S(2)}) collective-permute-start(bf16[192,768]{1,0:T(8,128)(2,1)S(1)} %collective-permute-done.3), channel_id=1, source_target_pairs={{0,1},{1,2},{2,3},{3,4},{4,5},{5,6},{6,7},{7,0},{8,9},{9,10},{10,1... | collective-permute-start | bytes 884744 | tf_op jit(solution)/shard_map/ppermute | solution.py:54
  59.5 18.9 %collective-permute-start.32 = (bf16[192,768]{1,0:T(8,128)(2,1)S(1)}, bf16[192,768]{1,0:T(8,128)(2,1)S(1)}, u32[]{:S(2)}, u32[]{:S(2)}) collective-permute-start(bf16[192,768]{1,0:T(8,128)(2,1)S(1)} %collective-permute-done.31), channel_id=1, source_target_pairs={{0,7},{1,0},{2,1},{3,2},{4,3},{5,4},{6,5},{7,6},{8,15},{9,8},{10,9... | collective-permute-start | bytes 884744 | tf_op jit(solution)/shard_map/ppermute | solution.py:55
  65.8 19.0 %collective-permute-start.12 = (bf16[192,768]{1,0:T(8,128)(2,1)S(1)}, bf16[192,768]{1,0:T(8,128)(2,1)S(1)}, u32[]{:S(2)}, u32[]{:S(2)}) collective-permute-start(bf16[192,768]{1,0:T(8,128)(2,1)S(1)} %collective-permute-done.11), channel_id=1, source_target_pairs={{0,7},{1,0},{2,1},{3,2},{4,3},{5,4},{6,5},{7,6},{8,15},{9,8},{10,9... | collective-permute-start | bytes 884744 | tf_op jit(solution)/shard_map/ppermute | solution.py:55
  69.3 21.7 %collective-permute-start.2 = (bf16[192,768]{1,0:T(8,128)(2,1)S(1)}, bf16[192,768]{1,0:T(8,128)(2,1)S(1)}, u32[]{:S(2)}, u32[]{:S(2)}) collective-permute-start(bf16[192,768]{1,0:T(8,128)(2,1)S(1)} %collective-permute-done.1), channel_id=1, source_target_pairs={{0,7},{1,0},{2,1},{3,2},{4,3},{5,4},{6,5},{7,6},{8,15},{9,8},{10,9... | collective-permute-start | bytes 884744 | tf_op jit(solution)/shard_map/ppermute | solution.py:55
  78.4 16.2 %collective-permute-start.5 = (bf16[192,768]{1,0:T(8,128)(2,1)S(1)}, bf16[192,768]{1,0:T(8,128)(2,1)S(1)}, u32[]{:S(2)}, u32[]{:S(2)}) collective-permute-start(bf16[192,768]{1,0:T(8,128)(2,1)S(1)} %collective-permute-done.4), channel_id=1, source_target_pairs={{0,1},{1,2},{2,3},{3,4},{4,5},{5,6},{6,7},{7,0},{8,9},{9,10},{10,1... | collective-permute-start | bytes 884744 | tf_op jit(solution)/shard_map/ppermute | solution.py:55
  91.0 16.3 %collective-permute-start.36 = (bf16[96,768]{1,0:T(8,128)(2,1)S(1)}, bf16[96,768]{1,0:T(8,128)(2,1)S(1)}, u32[]{:S(2)}, u32[]{:S(2)}) collective-permute-start(bf16[96,768]{1,0:T(8,128)(2,1)S(1)} %slice.322), channel_id=1, source_target_pairs={{0,1},{1,2},{2,3},{3,4},{4,5},{5,6},{6,7},{7,0},{8,9},{9,10},{10,1... | collective-permute-start | bytes 442376 | tf_op jit(solution)/shard_map/ppermute | solution.py:56
  91.1 19.6 %collective-permute-start.37 = (bf16[96,768]{1,0:T(8,128)(2,1)S(1)}, bf16[96,768]{1,0:T(8,128)(2,1)S(1)}, u32[]{:S(2)}, u32[]{:S(2)}) collective-permute-start(bf16[96,768]{1,0:T(8,128)(2,1)S(1)} %slice.323), channel_id=1, source_target_pairs={{0,7},{1,0},{2,1},{3,2},{4,3},{5,4},{6,5},{7,6},{8,15},{9,8},{10,9... | collective-permute-start | bytes 442376 | tf_op jit(solution)/shard_map/ppermute | solution.py:56
  94.6 16.7 %collective-permute-start.16 = (bf16[96,768]{1,0:T(8,128)(2,1)S(1)}, bf16[96,768]{1,0:T(8,128)(2,1)S(1)}, u32[]{:S(2)}, u32[]{:S(2)}) collective-permute-start(bf16[96,768]{1,0:T(8,128)(2,1)S(1)} %slice.310), channel_id=1, source_target_pairs={{0,1},{1,2},{2,3},{3,4},{4,5},{5,6},{6,7},{7,0},{8,9},{9,10},{10,1... | collective-permute-start | bytes 442376 | tf_op jit(solution)/shard_map/ppermute | solution.py:56
  95.9 16.2 %collective-permute-start.17 = (bf16[96,768]{1,0:T(8,128)(2,1)S(1)}, bf16[96,768]{1,0:T(8,128)(2,1)S(1)}, u32[]{:S(2)}, u32[]{:S(2)}) collective-permute-start(bf16[96,768]{1,0:T(8,128)(2,1)S(1)} %slice.311), channel_id=1, source_target_pairs={{0,7},{1,0},{2,1},{3,2},{4,3},{5,4},{6,5},{7,6},{8,15},{9,8},{10,9... | collective-permute-start | bytes 442376 | tf_op jit(solution)/shard_map/ppermute | solution.py:56
  144.1 16.8 %collective-permute-start.39 = (f32[128,768]{1,0:T(8,128)}, f32[128,768]{1,0:T(8,128)}, u32[]{:S(2)}, u32[]{:S(2)}) collective-permute-start(f32[128,768]{1,0:T(8,128)} %slice.327), channel_id=1, source_target_pairs={{0,128},{64,192},{128,0},{192,64},{1,129},{65,193},{129,1},{193,65... | collective-permute-start | bytes 1179656 | tf_op jit(solution)/shard_map/ppermute | solution.py:60
  145.0 24.3 %collective-permute-start.19 = (f32[128,768]{1,0:T(8,128)}, f32[128,768]{1,0:T(8,128)}, u32[]{:S(2)}, u32[]{:S(2)}) collective-permute-start(f32[128,768]{1,0:T(8,128)} %slice.315), channel_id=1, source_target_pairs={{0,128},{64,192},{128,0},{192,64},{1,129},{65,193},{129,1},{193,65... | collective-permute-start | bytes 1179656 | tf_op jit(solution)/shard_map/ppermute | solution.py:60
  148.8 28.9 %collective-permute-start.9 = (f32[128,768]{1,0:T(8,128)}, f32[128,768]{1,0:T(8,128)}, u32[]{:S(2)}, u32[]{:S(2)}) collective-permute-start(f32[128,768]{1,0:T(8,128)} %slice.309), channel_id=1, source_target_pairs={{0,128},{64,192},{128,0},{192,64},{1,129},{65,193},{129,1},{193,65... | collective-permute-start | bytes 1179656 | tf_op jit(solution)/shard_map/ppermute | solution.py:60
  192.5 16.2 %collective-permute-start.43 = (bf16[256,768]{1,0:T(8,128)(2,1)S(1)}, bf16[256,768]{1,0:T(8,128)(2,1)S(1)}, u32[]{:S(2)}, u32[]{:S(2)}) collective-permute-start(bf16[256,768]{1,0:T(8,128)(2,1)S(1)} %pad_maximum_fusion.10), channel_id=1, source_target_pairs={{0,64},{64,0},{128,192},{192,128},{1,65},{65,1},{129,193},{193,129... | collective-permute-start | bytes 1179656 | tf_op jit(solution)/shard_map/ppermute | solution.py:65
  200.9 17.2 %collective-permute-start.47 = (bf16[256,768]{1,0:T(8,128)(2,1)S(1)}, bf16[256,768]{1,0:T(8,128)(2,1)S(1)}, u32[]{:S(2)}, u32[]{:S(2)}) collective-permute-start(bf16[256,768]{1,0:T(8,128)(2,1)S(1)} %pad_maximum_fusion.12), channel_id=1, source_target_pairs={{0,64},{64,0},{128,192},{192,128},{1,65},{65,1},{129,193},{193,129... | collective-permute-start | bytes 1179656 | tf_op jit(solution)/shard_map/ppermute | solution.py:65
  203.5 29.0 %collective-permute-start.48 = (bf16[96,768]{1,0:T(8,128)(2,1)}, bf16[96,768]{1,0:T(8,128)(2,1)}, u32[]{:S(2)}, u32[]{:S(2)}) collective-permute-start(bf16[96,768]{1,0:T(8,128)(2,1)} %get-tuple-element.37), channel_id=1, source_target_pairs={{0,1},{1,2},{2,3},{3,4},{4,5},{5,6},{6,7},{7,0},{8,9},{9,10},{10,1... | collective-permute-start | bytes 442376 | tf_op jit(solution)/shard_map/ppermute | solution.py:74
  204.8 31.4 %collective-permute-start.52 = (bf16[96,768]{1,0:T(8,128)(2,1)}, bf16[96,768]{1,0:T(8,128)(2,1)}, u32[]{:S(2)}, u32[]{:S(2)}) collective-permute-start(bf16[96,768]{1,0:T(8,128)(2,1)} %get-tuple-element.38), channel_id=1, source_target_pairs={{0,7},{1,0},{2,1},{3,2},{4,3},{5,4},{6,5},{7,6},{8,15},{9,8},{10,9... | collective-permute-start | bytes 442376 | tf_op jit(solution)/shard_map/ppermute | solution.py:74
  209.8 27.6 %collective-permute-start.56 = (bf16[96,768]{1,0:T(8,128)(2,1)}, bf16[96,768]{1,0:T(8,128)(2,1)}, u32[]{:S(2)}, u32[]{:S(2)}) collective-permute-start(bf16[96,768]{1,0:T(8,128)(2,1)} %get-tuple-element.39), channel_id=1, source_target_pairs={{0,1},{1,2},{2,3},{3,4},{4,5},{5,6},{6,7},{7,0},{8,9},{9,10},{10,1... | collective-permute-start | bytes 442376 | tf_op jit(solution)/shard_map/ppermute | solution.py:74
  212.5 28.5 %collective-permute-start.60 = (bf16[96,768]{1,0:T(8,128)(2,1)}, bf16[96,768]{1,0:T(8,128)(2,1)}, u32[]{:S(2)}, u32[]{:S(2)}) collective-permute-start(bf16[96,768]{1,0:T(8,128)(2,1)} %get-tuple-element.40), channel_id=1, source_target_pairs={{0,7},{1,0},{2,1},{3,2},{4,3},{5,4},{6,5},{7,6},{8,15},{9,8},{10,9... | collective-permute-start | bytes 442376 | tf_op jit(solution)/shard_map/ppermute | solution.py:74
  218.2 24.2 %collective-permute-start.64 = (bf16[96,768]{1,0:T(8,128)(2,1)}, bf16[96,768]{1,0:T(8,128)(2,1)}, u32[]{:S(2)}, u32[]{:S(2)}) collective-permute-start(bf16[96,768]{1,0:T(8,128)(2,1)} %get-tuple-element.41), channel_id=1, source_target_pairs={{0,1},{1,2},{2,3},{3,4},{4,5},{5,6},{6,7},{7,0},{8,9},{9,10},{10,1... | collective-permute-start | bytes 442376 | tf_op jit(solution)/shard_map/ppermute | solution.py:74
  252.4 16.4 %collective-permute-start.73 = (bf16[192,768]{1,0:T(8,128)(2,1)S(1)}, bf16[192,768]{1,0:T(8,128)(2,1)S(1)}, u32[]{:S(2)}, u32[]{:S(2)}) collective-permute-start(bf16[192,768]{1,0:T(8,128)(2,1)S(1)} %pad_maximum_fusion.19), channel_id=1, source_target_pairs={{0,1},{1,2},{2,3},{3,4},{4,5},{5,6},{6,7},{7,0},{8,9},{9,10},{10,1... | collective-permute-start | bytes 884744 | tf_op jit(solution)/shard_map/ppermute | solution.py:78
  256.6 18.5 %collective-permute-start.50 = (bf16[192,768]{1,0:T(8,128)(2,1)S(1)}, bf16[192,768]{1,0:T(8,128)(2,1)S(1)}, u32[]{:S(2)}, u32[]{:S(2)}) collective-permute-start(bf16[192,768]{1,0:T(8,128)(2,1)S(1)} %fusion.11), channel_id=1, source_target_pairs={{0,1},{1,2},{2,3},{3,4},{4,5},{5,6},{6,7},{7,0},{8,9},{9,10},{10,1... | collective-permute-start | bytes 884744 | tf_op jit(solution)/shard_map/ppermute | solution.py:80
  262.9 18.5 %collective-permute-start.58 = (bf16[192,768]{1,0:T(8,128)(2,1)S(1)}, bf16[192,768]{1,0:T(8,128)(2,1)S(1)}, u32[]{:S(2)}, u32[]{:S(2)}) collective-permute-start(bf16[192,768]{1,0:T(8,128)(2,1)S(1)} %fusion.15), channel_id=1, source_target_pairs={{0,1},{1,2},{2,3},{3,4},{4,5},{5,6},{6,7},{7,0},{8,9},{9,10},{10,1... | collective-permute-start | bytes 884744 | tf_op jit(solution)/shard_map/ppermute | solution.py:80
  269.2 18.5 %collective-permute-start.66 = (bf16[192,768]{1,0:T(8,128)(2,1)S(1)}, bf16[192,768]{1,0:T(8,128)(2,1)S(1)}, u32[]{:S(2)}, u32[]{:S(2)}) collective-permute-start(bf16[192,768]{1,0:T(8,128)(2,1)S(1)} %fusion.19), channel_id=1, source_target_pairs={{0,1},{1,2},{2,3},{3,4},{4,5},{5,6},{6,7},{7,0},{8,9},{9,10},{10,1... | collective-permute-start | bytes 884744 | tf_op jit(solution)/shard_map/ppermute | solution.py:80
  275.6 18.4 %collective-permute-start.74 = (bf16[192,768]{1,0:T(8,128)(2,1)S(1)}, bf16[192,768]{1,0:T(8,128)(2,1)S(1)}, u32[]{:S(2)}, u32[]{:S(2)}) collective-permute-start(bf16[192,768]{1,0:T(8,128)(2,1)S(1)} %fusion.23), channel_id=1, source_target_pairs={{0,1},{1,2},{2,3},{3,4},{4,5},{5,6},{6,7},{7,0},{8,9},{9,10},{10,1... | collective-permute-start | bytes 884744 | tf_op jit(solution)/shard_map/ppermute | solution.py:80
  281.8 18.5 %collective-permute-start.51 = (bf16[192,768]{1,0:T(8,128)(2,1)S(1)}, bf16[192,768]{1,0:T(8,128)(2,1)S(1)}, u32[]{:S(2)}, u32[]{:S(2)}) collective-permute-start(bf16[192,768]{1,0:T(8,128)(2,1)S(1)} %fusion.10), channel_id=1, source_target_pairs={{0,1},{1,2},{2,3},{3,4},{4,5},{5,6},{6,7},{7,0},{8,9},{9,10},{10,1... | collective-permute-start | bytes 884744 | tf_op jit(solution)/shard_map/ppermute | solution.py:82
  288.2 18.5 %collective-permute-start.59 = (bf16[192,768]{1,0:T(8,128)(2,1)S(1)}, bf16[192,768]{1,0:T(8,128)(2,1)S(1)}, u32[]{:S(2)}, u32[]{:S(2)}) collective-permute-start(bf16[192,768]{1,0:T(8,128)(2,1)S(1)} %fusion.14), channel_id=1, source_target_pairs={{0,1},{1,2},{2,3},{3,4},{4,5},{5,6},{6,7},{7,0},{8,9},{9,10},{10,1... | collective-permute-start | bytes 884744 | tf_op jit(solution)/shard_map/ppermute | solution.py:82
  294.5 18.5 %collective-permute-start.67 = (bf16[192,768]{1,0:T(8,128)(2,1)S(1)}, bf16[192,768]{1,0:T(8,128)(2,1)S(1)}, u32[]{:S(2)}, u32[]{:S(2)}) collective-permute-start(bf16[192,768]{1,0:T(8,128)(2,1)S(1)} %fusion.18), channel_id=1, source_target_pairs={{0,1},{1,2},{2,3},{3,4},{4,5},{5,6},{6,7},{7,0},{8,9},{9,10},{10,1... | collective-permute-start | bytes 884744 | tf_op jit(solution)/shard_map/ppermute | solution.py:82
  300.3 19.0 %collective-permute-start.75 = (bf16[192,768]{1,0:T(8,128)(2,1)S(1)}, bf16[192,768]{1,0:T(8,128)(2,1)S(1)}, u32[]{:S(2)}, u32[]{:S(2)}) collective-permute-start(bf16[192,768]{1,0:T(8,128)(2,1)S(1)} %fusion.22), channel_id=1, source_target_pairs={{0,1},{1,2},{2,3},{3,4},{4,5},{5,6},{6,7},{7,0},{8,9},{9,10},{10,1... | collective-permute-start | bytes 884744 | tf_op jit(solution)/shard_map/ppermute | solution.py:82
  (99 other events, 1142.7 us)
Sparse Core Ops, SparseCore 0:
  27.0 38.3 all-gather.1
  231.2 43.8 reduce-scatter.1
